TPU v7x, 32 devices: a whole 2x2x4 slice. The times are simulated.
32 devices in a mesh: tile: 8 (over y, x, core), src: 4 (over z).
Axes of the slice: x: 2, y: 2, z: 4, core: 2. Of those that a mesh axis runs over, the one named last changes fastest.
Arguments:
- mask_tiles: int32 [128, 512], P('tile'), may hold values 0 or 1
- kernels: bfloat16 [16, 3, 8, 2, 17, 17], P('src'), may hold values from -0.5 to 0.5
- source_weight: int32 [16], P('src'), may hold values from 1 to 8
- dill_rate: float32 [8], P('src'), may hold values from 0.3 to 3
- quencher_load: float32 [8], P('src'), may hold values from 0.1 to 0.5
Outputs:
- acid_field: float32 [8, 128, 512], P('src', 'tile')
- inhibitor: float32 [8, 128, 512], P('src', 'tile')
All inputs are finite; a program needn't handle non-finite values. No bound on the sum of `mask_tiles` on one device may be relied on, other than what follows from the above.
Results may differ from a plain program's by a relative error of at most 0.0008.
Values may be sent and summed in bfloat16 or wider, within the bound.
A program may use at most 64 MiB of HBM per device.

v0:
```python
import functools

import jax
import jax.numpy as jnp
from jax import lax
from jax.experimental import pallas as pl
from jax.experimental.pallas import tpu as pltpu
from jax.sharding import PartitionSpec as P

STEPS = 8
SLAB = 24
DEEP = 512
MARGIN = 64

acid_lateral = 0.15
acid_vertical = 0.12
quench_lateral = 0.05
quench_vertical = 0.04
react_rate = 0.3
deprotect_rate = 0.25

MESH = pl.DeviceIdType.MESH


def kernel(
    dims,
    mask_ref, filt_ref, load_ref, dill_ref, acid_ref, inhib_ref,
    above, below, filters, loads, shifted, light, light_out, light_in,
    acid, quench, dose, final_out, final_in,
    mask_send, mask_recv, filt_send, filt_recv, load_send, load_recv,
    light_send, light_recv, final_send, final_recv,
):
    tiles, srcs, rows, cols, side, planes, scale = dims
    rim = side // 2
    halo = STEPS
    tall = rows + 2 * halo
    block = cols // srcs
    wide = block + 2 * MARGIN
    tile = lax.axis_index("tile")
    src = lax.axis_index("src")
    has_above = tile > 0
    has_below = tile < tiles - 1

    barrier = pltpu.get_barrier_semaphore()
    peers = [lax.rem(src + step, srcs) for step in range(1, srcs)]
    for peer in peers:
        pl.semaphore_signal(barrier, inc=1, device_id=(tile, peer), device_id_type=MESH)

    @pl.when(has_above)
    def _():
        pl.semaphore_signal(barrier, inc=1, device_id=(tile - 1, src), device_id_type=MESH)

    @pl.when(has_below)
    def _():
        pl.semaphore_signal(barrier, inc=1, device_id=(tile + 1, src), device_id_type=MESH)

    greeted = srcs - 1 + jnp.where(has_above, 1, 0) + jnp.where(has_below, 1, 0)
    pl.semaphore_wait(barrier, greeted)

    def to_above():
        return pltpu.make_async_remote_copy(
            mask_ref, below, mask_send.at[0], mask_recv.at[0],
            device_id=(tile - 1, src), device_id_type=MESH)

    def to_below():
        return pltpu.make_async_remote_copy(
            mask_ref, above, mask_send.at[1], mask_recv.at[1],
            device_id=(tile + 1, src), device_id_type=MESH)

    @pl.when(has_above)
    def _():
        to_above().start()

    @pl.when(has_below)
    def _():
        to_below().start()

    filt_copies = []
    load_copies = []
    for at, peer in enumerate(peers):
        copy = pltpu.make_async_remote_copy(
            filt_ref.at[peer], filters.at[src], filt_send.at[at], filt_recv.at[at],
            device_id=(tile, peer), device_id_type=MESH)
        copy.start()
        filt_copies.append(copy)
        copy = pltpu.make_async_remote_copy(
            load_ref, loads.at[src], load_send.at[at], load_recv.at[at],
            device_id=(tile, peer), device_id_type=MESH)
        copy.start()
        load_copies.append(copy)
    filters[src] = filt_ref[src]
    loads[src] = load_ref[...]
    shifted[...] = jnp.zeros_like(shifted)

    @pl.when(jnp.logical_not(has_above))
    def _():
        above[...] = jnp.zeros_like(above)

    @pl.when(jnp.logical_not(has_below))
    def _():
        below[...] = jnp.zeros_like(below)

    @pl.when(has_above)
    def _():
        to_above().wait_send()
        to_below().wait_recv()

    @pl.when(has_below)
    def _():
        to_below().wait_send()
        to_above().wait_recv()

    image = jnp.concatenate([above[...], mask_ref[...], below[...]], axis=0).astype(jnp.float32)
    ring = jnp.concatenate([image, jnp.zeros((image.shape[0], 128), jnp.float32)], axis=1)
    length = cols + 128
    for b in range(side):
        moved = pltpu.roll(ring, (rim - b) % length, 1)[:, :cols]
        for c in range(cols // 128):
            shifted[c, pl.ds(b, image.shape[0], SLAB), :] = moved[:, c * 128:(c + 1) * 128]

    for copy in filt_copies + load_copies:
        copy.wait()

    held = filters[...].reshape(-1, DEEP).astype(jnp.float32)
    lane = lax.broadcasted_iota(jnp.int32, held.shape, 1)
    weights = jnp.sum(jnp.where(lane == DEEP - 1, held, 0.0), axis=1, keepdims=True)
    taps = jnp.where(lane < side * SLAB, held, 0.0).astype(jnp.bfloat16)
    group = held.shape[0] // (srcs * planes)
    first = rows - halo - rim

    def one_row(r, carry):
        start = pl.multiple_of((r + first) * SLAB, 8)
        patch = jnp.concatenate(
            [shifted[c, pl.ds(start, DEEP), :] for c in range(cols // 128)], axis=1
        ).astype(jnp.bfloat16)
        field = jnp.dot(taps, patch, preferred_element_type=jnp.float32)
        power = (field * field * weights).reshape(srcs, planes, group, cols)
        for k in range(planes):
            light[k, pl.ds(r, 1), :] = jnp.sum(
                power[:, k].reshape(srcs * group, cols), axis=0, keepdims=True)
        return carry

    lax.fori_loop(0, tall, one_row, 0)

    for k in range(planes):
        exposed = light[k] * (dill_ref[k] * scale)
        exposed = jnp.concatenate([exposed, jnp.zeros((tall, 2 * MARGIN), jnp.float32)], axis=1)
        exposed = pltpu.roll(exposed, MARGIN, 1)
        for s in range(srcs):
            light_out[s, k] = exposed[:, s * block:s * block + wide].astype(jnp.bfloat16)
    light_in[src] = light_out[src]
    copies = []
    for at, peer in enumerate(peers):
        copy = pltpu.make_async_remote_copy(
            light_out.at[peer], light_in.at[src], light_send.at[at], light_recv.at[at],
            device_id=(tile, peer), device_id_type=MESH)
        copy.start()
        copies.append(copy)
    row = lax.broadcasted_iota(jnp.int32, (tall, wide), 0) + (tile * rows - halo)
    col = lax.broadcasted_iota(jnp.int32, (tall, wide), 1) + (src * block - MARGIN)
    inside = (row >= 0) & (row < tiles * rows) & (col >= 0) & (col < cols)
    inside = jnp.where(inside, 1.0, 0.0)
    for copy in copies:
        copy.wait()

    depth = srcs * planes
    for k in range(depth):
        exposed = light_in[k // planes, k % planes].astype(jnp.float32)
        acid[0, k] = (1.0 - jnp.exp(-exposed)) * inside
        quench[0, k] = loads[k // planes, k % planes:k % planes + 1, 0:1] * inside
        dose[k] = jnp.zeros((tall, wide), jnp.float32)

    def spread(held, now, k, lateral_rate, vertical_rate):
        centre = held[now, k]
        sides = (
            pltpu.roll(centre, 1, 0) + pltpu.roll(centre, tall - 1, 0)
            + pltpu.roll(centre, 1, 1) + pltpu.roll(centre, wide - 1, 1)
        )
        lateral = sides - 4.0 * centre
        vertical = held[now, min(k + 1, depth - 1)] + held[now, max(k - 1, 0)] - 2.0 * centre
        return centre, centre + lateral_rate * lateral + vertical_rate * vertical

    def two_steps(pair, carry):
        for now in range(2):
            for k in range(depth):
                a, a_next = spread(acid, now, k, acid_lateral, acid_vertical)
                q, q_next = spread(quench, now, k, quench_lateral, quench_vertical)
                reacted = react_rate * a * q
                a_next = (a_next - reacted) * inside
                acid[1 - now, k] = a_next
                quench[1 - now, k] = (q_next - reacted) * inside
                dose[k] = dose[k] + a_next
        return carry

    lax.fori_loop(0, STEPS // 2, two_steps, 0)

    for k in range(depth):
        for which, whole in enumerate((acid[0, k], jnp.exp(-deprotect_rate * dose[k]))):
            final_out[k // planes, which, k % planes] = pltpu.roll(
                whole, wide - MARGIN, 1)[halo:halo + rows, :block]
    copies = []
    for at, peer in enumerate(peers):
        copy = pltpu.make_async_remote_copy(
            final_out.at[peer], final_in.at[src], final_send.at[at], final_recv.at[at],
            device_id=(tile, peer), device_id_type=MESH)
        copy.start()
        copies.append(copy)
    final_in[src] = final_out[src]
    for copy in copies:
        copy.wait()
    for s in range(srcs):
        acid_ref[:, :, s * block:(s + 1) * block] = final_in[s, 0]
        inhib_ref[:, :, s * block:(s + 1) * block] = final_in[s, 1]


def shards(mask_tiles, kernels, source_weight, dill_rate, quencher_load):
    tiles, srcs = lax.axis_size("tile"), lax.axis_size("src")
    rows, cols = mask_tiles.shape
    planes = dill_rate.shape[0]
    points, parts, depth, quad, side, _ = kernels.shape
    group = points * parts * quad
    taps = jnp.pad(kernels, ((0, 0),) * 5 + ((0, SLAB - side),))
    taps = taps.reshape(points, parts, srcs, planes, quad, side * SLAB)
    spare = DEEP - side * SLAB
    last = jnp.arange(spare) == spare - 1
    tail = jnp.where(last, source_weight.astype(jnp.bfloat16)[:, None, None, None, None, None], 0)
    tail = jnp.broadcast_to(tail.astype(jnp.bfloat16), taps.shape[:-1] + (spare,))
    taps = jnp.concatenate([taps, tail], axis=-1)
    taps = taps.transpose(2, 3, 0, 1, 4, 5).reshape(srcs, planes * group, DEEP)
    loads = jnp.broadcast_to(jnp.pad(quencher_load, (0, 8 - planes))[:, None], (8, 128))
    dims = (tiles, srcs, rows, cols, side, planes, 1.0 / (24.0 * points * srcs))
    tall = rows + 2 * STEPS
    block = cols // srcs
    wide = block + 2 * MARGIN
    depth_all = srcs * planes
    f32 = jnp.float32
    image_rows = 3 * rows
    first = rows - STEPS - side // 2
    deep_rows = max(image_rows * SLAB, (first + tall - 1) * SLAB + DEEP)
    out = jax.ShapeDtypeStruct((planes, rows, cols), f32)
    vmem = pl.BlockSpec(memory_space=pltpu.VMEM)
    dma = pltpu.SemaphoreType.DMA
    return pl.pallas_call(
        functools.partial(kernel, dims),
        out_shape=(out, out),
        in_specs=[vmem, vmem, vmem, pl.BlockSpec(memory_space=pltpu.SMEM)],
        out_specs=(vmem, vmem),
        scratch_shapes=[
            pltpu.VMEM((rows, cols), jnp.int32),
            pltpu.VMEM((rows, cols), jnp.int32),
            pltpu.VMEM((srcs, planes * group, DEEP), jnp.bfloat16),
            pltpu.VMEM((srcs, 8, 128), f32),
            pltpu.VMEM((cols // 128, deep_rows, 128), f32),
            pltpu.VMEM((planes, tall, cols), f32),
            pltpu.VMEM((srcs, planes, tall, wide), jnp.bfloat16),
            pltpu.VMEM((srcs, planes, tall, wide), jnp.bfloat16),
            pltpu.VMEM((2, depth_all, tall, wide), f32),
            pltpu.VMEM((2, depth_all, tall, wide), f32),
            pltpu.VMEM((depth_all, tall, wide), f32),
            pltpu.VMEM((srcs, 2, planes, rows, block), f32),
            pltpu.VMEM((srcs, 2, planes, rows, block), f32),
            dma((2,)), dma((2,)),
            dma((srcs - 1,)), dma((srcs - 1,)),
            dma((srcs - 1,)), dma((srcs - 1,)),
            dma((srcs - 1,)), dma((srcs - 1,)),
            dma((srcs - 1,)), dma((srcs - 1,)),
        ],
        compiler_params=pltpu.CompilerParams(
            collective_id=0, has_side_effects=True, vmem_limit_bytes=40 * 1024 * 1024
        ),
    )(mask_tiles, taps, loads, dill_rate)


def solution(mesh):
    in_specs = (
        P("tile", None),
        P("src", None, None, None, None, None),
        P("src"),
        P("src"),
        P("src"),
    )
    out_specs = (P("src", "tile", None), P("src", "tile", None))
    return jax.shard_map(shards, mesh=mesh, in_specs=in_specs, out_specs=out_specs, check_vma=False)
```

profile of v0, /device:TPU:0, one launch (start us, length us, event | category | flops | bytes accessed | tf_op | source)
XLA Modules:
  0.0 37.8 jit_solution(3961173080115654496)
XLA Ops:
  0.6 1.4 %copy.9 = bf16[4,3,8,2,17,17]{5,4,3,2,1,0:T(8,128)(2,1)S(1)} copy(bf16[4,3,8,2,17,17]{5,3,4,2,1,0:T(2,128)(2,1)} %param.6) | data formatting | bytes 221952
  2.0 0.3 pad.8.clone
  2.4 0.0 copy-start.2
  2.4 0.0 copy-start.3
  2.4 0.0 copy-start
  2.4 0.0 copy-start.1
  2.4 0.8 %reshape.35 = bf16[4,3,4,2,2,408]{5,4,3,2,1,0:T(2,128)(2,1)S(1)} reshape(bf16[4,3,8,2,17,24]{5,4,3,2,1,0:T(8,128)(2,1)S(1)} %pad.8.clone) | data formatting | bytes 313344 | tf_op jit(solution)/shard_map/reshape | solution.py:223
  3.3 0.0 copy-done.2
  3.3 0.1 broadcast_select_fusion
  3.4 0.3 maximum_bitcast_fusion
  3.7 0.1 copy.8
  3.8 0.1 reshape.36.filt_ref
  3.9 0.0 copy-done.3
  4.0 0.1 broadcast_in_dim.32.load_ref
  4.0 0.0 copy-done
  4.0 0.0 copy-done.1
  4.0 32.5 %shard_map.68 = (f32[2,16,512]{2,1,0:T(8,128)S(1)}, f32[2,16,512]{2,1,0:T(8,128)S(1)}) custom-call(s32[16,512]{1,0:T(8,128)S(1)} %copy-done, bf16[4,48,512]{2,1,0:T(8,128)(2,1)S(1)} %reshape.36.filt_ref, f32[8,128]{1,0:T(8,128)S(1)} %broadcast_in_dim.32.load_ref, f32[2]{0:T(128)S(1)} %copy-done.1), custom_call_target="tpu_custom_call" | custom-call | tf_op jit(solution)/shard_map/pallas_call | solution.py:243
  36.6 0.6 %copy.12 = f32[2,16,512]{2,1,0:T(8,128)} copy(f32[2,16,512]{2,1,0:T(8,128)S(1)} %get-tuple-element.4) | data formatting | bytes 131072
  37.2 0.6 %copy.13 = f32[2,16,512]{2,1,0:T(8,128)} copy(f32[2,16,512]{2,1,0:T(8,128)S(1)} %get-tuple-element.5) | data formatting | bytes 131072
  (4 shorter events, 0.0 us)
Async XLA Ops:
  2.4 0.9 %copy-start.2 = (s32[4]{0:T(128)S(1)}, s32[4]{0:T(128)}, u32[]{:S(2)}) copy-start(s32[4]{0:T(128)} %param.7) | copy-start | bytes 52
  2.4 1.6 %copy-start.3 = (f32[2]{0:T(128)S(1)}, f32[2]{0:T(128)}, u32[]{:S(2)}) copy-start(f32[2]{0:T(128)} %param.9) | copy-start | bytes 28
  2.4 1.6 %copy-start = (s32[16,512]{1,0:T(8,128)S(1)}, s32[16,512]{1,0:T(8,128)}, u32[]{:S(2)}) copy-start(s32[16,512]{1,0:T(8,128)} %mask_ref.1) | copy-start | bytes 98308
  2.4 1.6 %copy-start.1 = (f32[2]{0:T(128)S(1)}, f32[2]{0:T(128)}, u32[]{:S(2)}) copy-start(f32[2]{0:T(128)} %dill_ref.1) | copy-start | bytes 28
where the time goes:
time: 38 us; the launch traced here: 37.8 us
  Pallas kernels  32.5 us (86%)
  local copies, waits for them, and re-layouts  4.18 us (11%)
  between operations  0.75 us (2%)
    pallas_call x1, Pallas kernels, shards(): pl.pallas_call(functools.partial(kernel, dims), out_shape=(out, out), in_...  32.5 us
    unnamed x11, local copies, waits for them, and re-layouts  2.69 us
    reshape x1, local copies, waits for them, and re-layouts, shards(): taps = taps.reshape(points, parts, srcs, planes, quad, side * SLAB)  0.84 us

commit v1 on v0

--- a/solution.py
+++ b/solution.py
@@ -8,8 +8,10 @@
 from jax.sharding import PartitionSpec as P
 
 STEPS = 8
-SLAB = 24
+SLAB = 21
 DEEP = 512
+WIRE = 384
+GROUP = 8
 MARGIN = 64
 
 acid_lateral = 0.15
@@ -24,8 +26,9 @@
 
 def kernel(
     dims,
-    mask_ref, filt_ref, load_ref, dill_ref, acid_ref, inhib_ref,
-    above, below, filters, loads, shifted, light, light_out, light_in,
+    mask_ref, raw_ref, pupil_ref, dill_ref, quench_ref, acid_ref, inhib_ref,
+    above, below, unsorted, sorted_rows, filt_out, load_out, filters, loads, shifted, patches, taps,
+    light, light_out, light_in,
     acid, quench, dose, final_out, final_in,
     mask_send, mask_recv, filt_send, filt_recv, load_send, load_recv,
     light_send, light_recv, final_send, final_recv,
@@ -54,6 +57,42 @@
     def _():
         pl.semaphore_signal(barrier, inc=1, device_id=(tile + 1, src), device_id_type=MESH)
 
+    lanes = 128
+    points, parts = pupil_ref.shape[0], raw_ref.shape[0] // (2 * side * srcs * planes * pupil_ref.shape[0])
+    channels = srcs * planes * points * parts
+    share = planes * points * parts
+    lane = lax.broadcasted_iota(jnp.int32, (channels, lanes), 1)
+    point = lax.broadcasted_iota(jnp.int32, (channels, lanes), 0) // (srcs * planes * parts)
+    weight = jnp.zeros((channels, lanes), jnp.float32)
+    for p in range(points):
+        weight = jnp.where(point == p, pupil_ref[p].astype(jnp.float32), weight)
+    weight = jnp.where(lane == lanes - 1, weight, 0.0)
+    for q in range(2):
+        strips = [jnp.zeros((channels, lanes), jnp.float32) for _ in range(WIRE // lanes)]
+        strips[-1] = weight
+        for a in range(side):
+            part = raw_ref[pl.ds(2 * a + q, channels, 2 * side), :]
+            at, offset = divmod(a * SLAB, lanes)
+            if offset:
+                part = pltpu.roll(part, offset, 1)
+            if offset + side > lanes:
+                strips[at + 1] = strips[at + 1] + jnp.where(lane < offset, part, 0.0)
+                part = jnp.where(lane >= offset, part, 0.0)
+            strips[at] = strips[at] + part
+        for c, strip in enumerate(strips):
+            unsorted[q, c] = strip
+            for k in range(srcs * planes):
+                sorted_rows[q, c, k * points * parts:(k + 1) * points * parts] = unsorted[
+                    q, c, pl.ds(k, points * parts, srcs * planes), :]
+            for s in range(srcs):
+                filt_out[s, q * share:(q + 1) * share, c * lanes:(c + 1) * lanes] = sorted_rows[
+                    q, c, s * share:(s + 1) * share].astype(jnp.bfloat16)
+    plane = lax.broadcasted_iota(jnp.int32, load_out.shape, 0)
+    spread_load = jnp.zeros(load_out.shape, jnp.float32)
+    for k in range(planes):
+        spread_load = jnp.where(plane == k, quench_ref[k], spread_load)
+    load_out[...] = spread_load
+
     greeted = srcs - 1 + jnp.where(has_above, 1, 0) + jnp.where(has_below, 1, 0)
     pl.semaphore_wait(barrier, greeted)
 
@@ -79,17 +118,17 @@
     load_copies = []
     for at, peer in enumerate(peers):
         copy = pltpu.make_async_remote_copy(
-            filt_ref.at[peer], filters.at[src], filt_send.at[at], filt_recv.at[at],
+            filt_out.at[peer], filters.at[src], filt_send.at[at], filt_recv.at[at],
             device_id=(tile, peer), device_id_type=MESH)
         copy.start()
         filt_copies.append(copy)
         copy = pltpu.make_async_remote_copy(
-            load_ref, loads.at[src], load_send.at[at], load_recv.at[at],
+            load_out, loads.at[src], load_send.at[at], load_recv.at[at],
             device_id=(tile, peer), device_id_type=MESH)
         copy.start()
         load_copies.append(copy)
-    filters[src] = filt_ref[src]
-    loads[src] = load_ref[...]
+    filters[src] = filt_out[src]
+    loads[src] = load_out[...]
     shifted[...] = jnp.zeros_like(shifted)
 
     @pl.when(jnp.logical_not(has_above))
@@ -118,29 +157,40 @@
         for c in range(cols // 128):
             shifted[c, pl.ds(b, image.shape[0], SLAB), :] = moved[:, c * 128:(c + 1) * 128]
 
-    for copy in filt_copies + load_copies:
+    for g in range(tall // GROUP):
+        for c in range(cols // 128):
+            patches[g, :, c * 128:(c + 1) * 128] = shifted[
+                c, g * GROUP * SLAB:g * GROUP * SLAB + DEEP, :].astype(jnp.bfloat16)
+    light[...] = jnp.zeros_like(light)
+
+    place = lax.broadcasted_iota(jnp.int32, (2 * share, WIRE), 1)
+    ours = lax.broadcasted_iota(jnp.int32, (share, cols), 0) // (points * parts)
+    for step in range(srcs):
+        if step:
+            filt_copies[step - 1].wait_recv()
+        held = filters[lax.rem(src + srcs - step, srcs)].astype(jnp.float32)
+        weights = jnp.sum(jnp.where(place == WIRE - 1, held, 0.0), axis=1, keepdims=True)[:share]
+        held = jnp.where(place < side * SLAB, held, 0.0)
+        held = jnp.concatenate([held, jnp.zeros((2 * share, DEEP - WIRE), jnp.float32)], axis=1)
+        for r in range(GROUP):
+            moved = pltpu.roll(held, r * SLAB, 1) if r else held
+            taps[r * 2 * share:(r + 1) * 2 * share] = moved.astype(jnp.bfloat16)
+
+        def one_group(g, carry):
+            field = jnp.dot(taps[...], patches[g], preferred_element_type=jnp.float32)
+            square = (field * field).reshape(GROUP, 2, share, cols)
+            power = (square[:, 0] + square[:, 1]) * weights
+            start = pl.multiple_of(g * GROUP, GROUP)
+            for k in range(planes):
+                own = jnp.where(ours == k, power, 0.0)
+                light[k, pl.ds(start, GROUP), :] += jnp.sum(own, axis=1)
+            return carry
+
+        lax.fori_loop(0, tall // GROUP, one_group, 0)
+    for copy in load_copies:
         copy.wait()
-
-    held = filters[...].reshape(-1, DEEP).astype(jnp.float32)
-    lane = lax.broadcasted_iota(jnp.int32, held.shape, 1)
-    weights = jnp.sum(jnp.where(lane == DEEP - 1, held, 0.0), axis=1, keepdims=True)
-    taps = jnp.where(lane < side * SLAB, held, 0.0).astype(jnp.bfloat16)
-    group = held.shape[0] // (srcs * planes)
-    first = rows - halo - rim
-
-    def one_row(r, carry):
-        start = pl.multiple_of((r + first) * SLAB, 8)
-        patch = jnp.concatenate(
-            [shifted[c, pl.ds(start, DEEP), :] for c in range(cols // 128)], axis=1
-        ).astype(jnp.bfloat16)
-        field = jnp.dot(taps, patch, preferred_element_type=jnp.float32)
-        power = (field * field * weights).reshape(srcs, planes, group, cols)
-        for k in range(planes):
-            light[k, pl.ds(r, 1), :] = jnp.sum(
-                power[:, k].reshape(srcs * group, cols), axis=0, keepdims=True)
-        return carry
-
-    lax.fori_loop(0, tall, one_row, 0)
+    for copy in filt_copies:
+        copy.wait_send()
 
     for k in range(planes):
         exposed = light[k] * (dill_ref[k] * scale)
@@ -176,9 +226,9 @@
             pltpu.roll(centre, 1, 0) + pltpu.roll(centre, tall - 1, 0)
             + pltpu.roll(centre, 1, 1) + pltpu.roll(centre, wide - 1, 1)
         )
-        lateral = sides - 4.0 * centre
-        vertical = held[now, min(k + 1, depth - 1)] + held[now, max(k - 1, 0)] - 2.0 * centre
-        return centre, centre + lateral_rate * lateral + vertical_rate * vertical
+        vertical = held[now, min(k + 1, depth - 1)] + held[now, max(k - 1, 0)]
+        stay = 1.0 - 4.0 * lateral_rate - 2.0 * vertical_rate
+        return centre, stay * centre + lateral_rate * sides + vertical_rate * vertical
 
     def two_steps(pair, carry):
         for now in range(2):
@@ -218,16 +268,9 @@
     rows, cols = mask_tiles.shape
     planes = dill_rate.shape[0]
     points, parts, depth, quad, side, _ = kernels.shape
-    group = points * parts * quad
-    taps = jnp.pad(kernels, ((0, 0),) * 5 + ((0, SLAB - side),))
-    taps = taps.reshape(points, parts, srcs, planes, quad, side * SLAB)
-    spare = DEEP - side * SLAB
-    last = jnp.arange(spare) == spare - 1
-    tail = jnp.where(last, source_weight.astype(jnp.bfloat16)[:, None, None, None, None, None], 0)
-    tail = jnp.broadcast_to(tail.astype(jnp.bfloat16), taps.shape[:-1] + (spare,))
-    taps = jnp.concatenate([taps, tail], axis=-1)
-    taps = taps.transpose(2, 3, 0, 1, 4, 5).reshape(srcs, planes * group, DEEP)
-    loads = jnp.broadcast_to(jnp.pad(quencher_load, (0, 8 - planes))[:, None], (8, 128))
+    share = planes * points * parts
+    raw = kernels.transpose(0, 1, 2, 4, 3, 5).astype(jnp.float32)
+    raw = jnp.pad(raw, ((0, 0),) * 5 + ((0, 128 - side),)).reshape(-1, 128)
     dims = (tiles, srcs, rows, cols, side, planes, 1.0 / (24.0 * points * srcs))
     tall = rows + 2 * STEPS
     block = cols // srcs
@@ -235,22 +278,28 @@
     depth_all = srcs * planes
     f32 = jnp.float32
     image_rows = 3 * rows
-    first = rows - STEPS - side // 2
-    deep_rows = max(image_rows * SLAB, (first + tall - 1) * SLAB + DEEP)
+    deep_rows = max(image_rows * SLAB, (tall - GROUP) * SLAB + DEEP)
     out = jax.ShapeDtypeStruct((planes, rows, cols), f32)
     vmem = pl.BlockSpec(memory_space=pltpu.VMEM)
+    smem = pl.BlockSpec(memory_space=pltpu.SMEM)
     dma = pltpu.SemaphoreType.DMA
     return pl.pallas_call(
         functools.partial(kernel, dims),
         out_shape=(out, out),
-        in_specs=[vmem, vmem, vmem, pl.BlockSpec(memory_space=pltpu.SMEM)],
+        in_specs=[vmem, vmem, smem, smem, smem],
         out_specs=(vmem, vmem),
         scratch_shapes=[
             pltpu.VMEM((rows, cols), jnp.int32),
             pltpu.VMEM((rows, cols), jnp.int32),
-            pltpu.VMEM((srcs, planes * group, DEEP), jnp.bfloat16),
+            pltpu.VMEM((2, WIRE // 128, srcs * share, 128), f32),
+            pltpu.VMEM((2, WIRE // 128, srcs * share, 128), f32),
+            pltpu.VMEM((srcs, 2 * share, WIRE), jnp.bfloat16),
+            pltpu.VMEM((8, 128), f32),
+            pltpu.VMEM((srcs, 2 * share, WIRE), jnp.bfloat16),
             pltpu.VMEM((srcs, 8, 128), f32),
             pltpu.VMEM((cols // 128, deep_rows, 128), f32),
+            pltpu.VMEM((tall // GROUP, DEEP, cols), jnp.bfloat16),
+            pltpu.VMEM((GROUP * 2 * share, DEEP), jnp.bfloat16),
             pltpu.VMEM((planes, tall, cols), f32),
             pltpu.VMEM((srcs, planes, tall, wide), jnp.bfloat16),
             pltpu.VMEM((srcs, planes, tall, wide), jnp.bfloat16),
@@ -268,7 +317,7 @@
         compiler_params=pltpu.CompilerParams(
             collective_id=0, has_side_effects=True, vmem_limit_bytes=40 * 1024 * 1024
         ),
-    )(mask_tiles, taps, loads, dill_rate)
+    )(mask_tiles, raw, source_weight, dill_rate, quencher_load)
 
 
 def solution(mesh):

time: 38 us -> 32.2 us (0.85)
  the two profiles are of different devices: /device:TPU:0 before, /device:TPU:4 now
where the time goes in v1:
time: 32.2 us; the launch traced here: 32 us
  Pallas kernels  27.3 us (85%)
  local copies, waits for them, and re-layouts  3.89 us (12%)
  between operations  0.68 us (2%)
    pallas_call x1, Pallas kernels, shards(): pl.pallas_call(functools.partial(kernel, dims), out_shape=(out, out), in_...  27.3 us
    pad x1, local copies, waits for them, and re-layouts, shards(): raw = jnp.pad(raw, ((0, 0),) * 5 + ((0, 128 - side),)).reshape(-1, 128)  2.02 us
    unnamed x10, local copies, waits for them, and re-layouts  1.88 us

profile of v1, /device:TPU:4, one launch (start us, length us, event | category | flops | bytes accessed | tf_op | source)
XLA Modules:
  0.0 32.0 jit_solution(3825355761480269459)
XLA Ops:
  0.6 2.0 %pad.5 = bf16[4,3,8,17,2,128]{5,4,3,2,1,0:T(2,128)(2,1)S(1)} pad(bf16[4,3,8,17,2,17]{5,4,3,2,1,0:T(2,128)(2,1)} %bitcast.4, bf16[]{:T(256)} %constant.3.clone.1), padding=0_0x0_0x0_0x0_0x0_0x0_111 | pad | bytes 946562 | tf_op jit(solution)/shard_map/jit(_pad)/pad | solution.py:273
  2.6 0.0 copy-start
  2.7 0.0 copy-start.1
  2.7 0.0 copy-start.2
  2.7 0.0 copy-start.3
  2.7 0.1 convert.4.raw_ref
  2.8 0.6 %copy-done = s32[16,512]{1,0:T(8,128)S(1)} copy-done((s32[16,512]{1,0:T(8,128)S(1)}, s32[16,512]{1,0:T(8,128)}, u32[]{:S(2)}) %copy-start) | copy-done | bytes 32792
  3.4 0.0 copy-done.1
  3.4 0.0 copy-done.2
  3.4 0.0 copy-done.3
  3.4 27.3 %shard_map.68 = (f32[2,16,512]{2,1,0:T(8,128)S(1)}, f32[2,16,512]{2,1,0:T(8,128)S(1)}) custom-call(s32[16,512]{1,0:T(8,128)S(1)} %copy-done, f32[3264,128]{1,0:T(8,128)S(1)} %convert.4.raw_ref, s32[4]{0:T(128)S(1)} %copy-done.1, f32[2]{0:T(128)S(1)} %copy-done.2, f32[2]{0:T(128)S(1)} %copy-done.3), custom_call_target="tpu_custom_call" | custom-call | tf_op jit(solution)/shard_map/pallas_call | solution.py:286
  30.7 0.6 %copy.9 = f32[2,16,512]{2,1,0:T(8,128)} copy(f32[2,16,512]{2,1,0:T(8,128)S(1)} %get-tuple-element.4) | data formatting | bytes 131072
  31.3 0.6 %copy.10 = f32[2,16,512]{2,1,0:T(8,128)} copy(f32[2,16,512]{2,1,0:T(8,128)S(1)} %get-tuple-element.5) | data formatting | bytes 131072
Async XLA Ops:
  2.6 0.8 %copy-start = (s32[16,512]{1,0:T(8,128)S(1)}, s32[16,512]{1,0:T(8,128)}, u32[]{:S(2)}) copy-start(s32[16,512]{1,0:T(8,128)} %mask_ref.1) | copy-start | bytes 98308
  2.7 0.8 %copy-start.1 = (s32[4]{0:T(128)S(1)}, s32[4]{0:T(128)}, u32[]{:S(2)}) copy-start(s32[4]{0:T(128)} %pupil_ref.1) | copy-start | bytes 52
  2.7 0.7 %copy-start.2 = (f32[2]{0:T(128)S(1)}, f32[2]{0:T(128)}, u32[]{:S(2)}) copy-start(f32[2]{0:T(128)} %dill_ref.1) | copy-start | bytes 28
  2.7 0.7 %copy-start.3 = (f32[2]{0:T(128)S(1)}, f32[2]{0:T(128)}, u32[]{:S(2)}) copy-start(f32[2]{0:T(128)} %quench_ref.1) | copy-start | bytes 28

commit v2 on v1

--- a/solution.py
+++ b/solution.py
@@ -12,7 +12,6 @@
 DEEP = 512
 WIRE = 384
 GROUP = 8
-MARGIN = 64
 
 acid_lateral = 0.15
 acid_vertical = 0.12
@@ -27,18 +26,18 @@
 def kernel(
     dims,
     mask_ref, raw_ref, pupil_ref, dill_ref, quench_ref, acid_ref, inhib_ref,
-    above, below, unsorted, sorted_rows, filt_out, load_out, filters, loads, shifted, patches, taps,
-    light, light_out, light_in,
+    above, below, raw, unsorted, sorted_rows, filt_out, load_out, filters, loads, shifted, patches, taps,
+    light, light_out, light_in, rim_out, rim_in,
     acid, quench, dose, final_out, final_in,
     mask_send, mask_recv, filt_send, filt_recv, load_send, load_recv,
-    light_send, light_recv, final_send, final_recv,
+    light_send, light_recv, rim_send, rim_recv, final_send, final_recv,
 ):
     tiles, srcs, rows, cols, side, planes, scale = dims
     rim = side // 2
     halo = STEPS
     tall = rows + 2 * halo
     block = cols // srcs
-    wide = block + 2 * MARGIN
+    wide = block + 128
     tile = lax.axis_index("tile")
     src = lax.axis_index("src")
     has_above = tile > 0
@@ -67,11 +66,19 @@
     for p in range(points):
         weight = jnp.where(point == p, pupil_ref[p].astype(jnp.float32), weight)
     weight = jnp.where(lane == lanes - 1, weight, 0.0)
+    raw[...] = jnp.zeros_like(raw)
+
+    def widen(at, carry):
+        here = pl.ds(pl.multiple_of(at * channels, channels), channels)
+        raw[here, :side] = raw_ref[here, :].astype(jnp.float32)
+        return carry
+
+    lax.fori_loop(0, 2 * side, widen, 0)
     for q in range(2):
         strips = [jnp.zeros((channels, lanes), jnp.float32) for _ in range(WIRE // lanes)]
         strips[-1] = weight
         for a in range(side):
-            part = raw_ref[pl.ds(2 * a + q, channels, 2 * side), :]
+            part = raw[pl.ds(2 * a + q, channels, 2 * side), :]
             at, offset = divmod(a * SLAB, lanes)
             if offset:
                 part = pltpu.roll(part, offset, 1)
@@ -192,13 +199,22 @@
     for copy in filt_copies:
         copy.wait_send()
 
+    edge = lax.broadcasted_iota(jnp.int32, (GROUP, 128), 1)
+    none = jnp.zeros((GROUP, 128), jnp.float32)
+    rims = [none] * srcs
     for k in range(planes):
         exposed = light[k] * (dill_ref[k] * scale)
-        exposed = jnp.concatenate([exposed, jnp.zeros((tall, 2 * MARGIN), jnp.float32)], axis=1)
-        exposed = pltpu.roll(exposed, MARGIN, 1)
         for s in range(srcs):
-            light_out[s, k] = exposed[:, s * block:s * block + wide].astype(jnp.bfloat16)
-    light_in[src] = light_out[src]
+            light_out[s, k] = exposed[:, s * block:(s + 1) * block].astype(jnp.bfloat16)
+            for g in range(tall // GROUP):
+                rows8 = exposed[g * GROUP:(g + 1) * GROUP]
+                right = rows8[:, (s + 1) * block:(s + 1) * block + 128] if s < srcs - 1 else none
+                left = rows8[:, s * block - 128:s * block] if s else none
+                picked = jnp.where(edge < halo, right, jnp.where(edge >= 128 - halo, left, 0.0))
+                shift = 2 * halo * (k * (tall // GROUP) + g)
+                rims[s] = rims[s] + (pltpu.roll(picked, shift, 1) if shift else picked)
+    for s in range(srcs):
+        rim_out[s] = rims[s]
     copies = []
     for at, peer in enumerate(peers):
         copy = pltpu.make_async_remote_copy(
@@ -206,8 +222,16 @@
             device_id=(tile, peer), device_id_type=MESH)
         copy.start()
         copies.append(copy)
+        copy = pltpu.make_async_remote_copy(
+            rim_out.at[peer], rim_in.at[src], rim_send.at[at], rim_recv.at[at],
+            device_id=(tile, peer), device_id_type=MESH)
+        copy.start()
+        copies.append(copy)
+    light_in[src] = light_out[src]
+    rim_in[src] = rim_out[src]
     row = lax.broadcasted_iota(jnp.int32, (tall, wide), 0) + (tile * rows - halo)
-    col = lax.broadcasted_iota(jnp.int32, (tall, wide), 1) + (src * block - MARGIN)
+    col = lax.broadcasted_iota(jnp.int32, (tall, wide), 1)
+    col = src * block + jnp.where(col < block + 64, col, col - wide)
     inside = (row >= 0) & (row < tiles * rows) & (col >= 0) & (col < cols)
     inside = jnp.where(inside, 1.0, 0.0)
     for copy in copies:
@@ -215,10 +239,20 @@
 
     depth = srcs * planes
     for k in range(depth):
-        exposed = light_in[k // planes, k % planes].astype(jnp.float32)
+        sent = rim_in[k // planes]
+        rim = []
+        for g in range(tall // GROUP):
+            shift = 2 * halo * (k % planes * (tall // GROUP) + g)
+            rim.append(pltpu.roll(sent, 128 - shift, 1) if shift else sent)
+        exposed = jnp.concatenate(
+            [light_in[k // planes, k % planes].astype(jnp.float32), jnp.concatenate(rim, axis=0)], axis=1)
         acid[0, k] = (1.0 - jnp.exp(-exposed)) * inside
         quench[0, k] = loads[k // planes, k % planes:k % planes + 1, 0:1] * inside
-        dose[k] = jnp.zeros((tall, wide), jnp.float32)
+        dose[k] = jnp.zeros((rows, block), jnp.float32)
+
+    def blend(centre, sides, vertical, lateral_rate, vertical_rate):
+        stay = 1.0 - 4.0 * lateral_rate - 2.0 * vertical_rate
+        return stay * centre + lateral_rate * sides + vertical_rate * vertical
 
     def spread(held, now, k, lateral_rate, vertical_rate):
         centre = held[now, k]
@@ -227,37 +261,60 @@
             + pltpu.roll(centre, 1, 1) + pltpu.roll(centre, wide - 1, 1)
         )
         vertical = held[now, min(k + 1, depth - 1)] + held[now, max(k - 1, 0)]
-        stay = 1.0 - 4.0 * lateral_rate - 2.0 * vertical_rate
-        return centre, stay * centre + lateral_rate * sides + vertical_rate * vertical
+        return centre, blend(centre, sides, vertical, lateral_rate, vertical_rate)
+
+    def one_step(now):
+        for k in range(depth):
+            a, a_next = spread(acid, now, k, acid_lateral, acid_vertical)
+            q, q_next = spread(quench, now, k, quench_lateral, quench_vertical)
+            reacted = react_rate * a * q
+            a_next = (a_next - reacted) * inside
+            acid[1 - now, k] = a_next
+            quench[1 - now, k] = (q_next - reacted) * inside
+            dose[k] = dose[k] + a_next[halo:halo + rows, :block]
 
     def two_steps(pair, carry):
-        for now in range(2):
-            for k in range(depth):
-                a, a_next = spread(acid, now, k, acid_lateral, acid_vertical)
-                q, q_next = spread(quench, now, k, quench_lateral, quench_vertical)
-                reacted = react_rate * a * q
-                a_next = (a_next - reacted) * inside
-                acid[1 - now, k] = a_next
-                quench[1 - now, k] = (q_next - reacted) * inside
-                dose[k] = dose[k] + a_next
+        one_step(0)
+        one_step(1)
         return carry
 
-    lax.fori_loop(0, STEPS // 2, two_steps, 0)
-
-    for k in range(depth):
-        for which, whole in enumerate((acid[0, k], jnp.exp(-deprotect_rate * dose[k]))):
-            final_out[k // planes, which, k % planes] = pltpu.roll(
-                whole, wide - MARGIN, 1)[halo:halo + rows, :block]
-    copies = []
-    for at, peer in enumerate(peers):
-        copy = pltpu.make_async_remote_copy(
-            final_out.at[peer], final_in.at[src], final_send.at[at], final_recv.at[at],
-            device_id=(tile, peer), device_id_type=MESH)
-        copy.start()
-        copies.append(copy)
-    final_in[src] = final_out[src]
-    for copy in copies:
-        copy.wait()
+    lax.fori_loop(0, STEPS // 2 - 1, two_steps, 0)
+    one_step(0)
+
+    def final_copy(s, slot):
+        return pltpu.make_async_remote_copy(
+            final_out.at[s], final_in.at[slot], final_send.at[s], final_recv.at[slot],
+            device_id=(tile, s), device_id_type=MESH)
+
+    own = slice(halo, halo + rows)
+    for s in range(srcs):
+        for k in range(s * planes, (s + 1) * planes):
+            strip = acid[1, k, own]
+            centre = strip[:, :block]
+            sides = (
+                acid[1, k, halo - 1:halo + rows - 1, :block] + acid[1, k, halo + 1:halo + rows + 1, :block]
+                + pltpu.roll(strip, 1, 1)[:, :block] + pltpu.roll(strip, wide - 1, 1)[:, :block]
+            )
+            vertical = acid[1, min(k + 1, depth - 1), own, :block] + acid[1, max(k - 1, 0), own, :block]
+            reacted = react_rate * centre * quench[1, k, own, :block]
+            a_next = blend(centre, sides, vertical, acid_lateral, acid_vertical) - reacted
+            final_out[s, 0, k % planes] = a_next
+            final_out[s, 1, k % planes] = jnp.exp(-deprotect_rate * (dose[k] + a_next))
+
+        @pl.when(src != s)
+        def _():
+            final_copy(s, src).start()
+
+        @pl.when(src == s)
+        def _():
+            final_in[s] = final_out[s]
+
+    for s in range(srcs):
+        @pl.when(src != s)
+        def _():
+            final_copy(s, src).wait_send()
+            final_copy(s, s).wait_recv()
+
     for s in range(srcs):
         acid_ref[:, :, s * block:(s + 1) * block] = final_in[s, 0]
         inhib_ref[:, :, s * block:(s + 1) * block] = final_in[s, 1]
@@ -269,12 +326,11 @@
     planes = dill_rate.shape[0]
     points, parts, depth, quad, side, _ = kernels.shape
     share = planes * points * parts
-    raw = kernels.transpose(0, 1, 2, 4, 3, 5).astype(jnp.float32)
-    raw = jnp.pad(raw, ((0, 0),) * 5 + ((0, 128 - side),)).reshape(-1, 128)
+    raw = kernels.transpose(0, 1, 2, 4, 3, 5).reshape(-1, side)
     dims = (tiles, srcs, rows, cols, side, planes, 1.0 / (24.0 * points * srcs))
     tall = rows + 2 * STEPS
     block = cols // srcs
-    wide = block + 2 * MARGIN
+    wide = block + 128
     depth_all = srcs * planes
     f32 = jnp.float32
     image_rows = 3 * rows
@@ -291,6 +347,7 @@
         scratch_shapes=[
             pltpu.VMEM((rows, cols), jnp.int32),
             pltpu.VMEM((rows, cols), jnp.int32),
+            pltpu.VMEM((raw.shape[0], 128), f32),
             pltpu.VMEM((2, WIRE // 128, srcs * share, 128), f32),
             pltpu.VMEM((2, WIRE // 128, srcs * share, 128), f32),
             pltpu.VMEM((srcs, 2 * share, WIRE), jnp.bfloat16),
@@ -301,11 +358,13 @@
             pltpu.VMEM((tall // GROUP, DEEP, cols), jnp.bfloat16),
             pltpu.VMEM((GROUP * 2 * share, DEEP), jnp.bfloat16),
             pltpu.VMEM((planes, tall, cols), f32),
-            pltpu.VMEM((srcs, planes, tall, wide), jnp.bfloat16),
-            pltpu.VMEM((srcs, planes, tall, wide), jnp.bfloat16),
+            pltpu.VMEM((srcs, planes, tall, block), jnp.bfloat16),
+            pltpu.VMEM((srcs, planes, tall, block), jnp.bfloat16),
+            pltpu.VMEM((srcs, GROUP, 128), f32),
+            pltpu.VMEM((srcs, GROUP, 128), f32),
             pltpu.VMEM((2, depth_all, tall, wide), f32),
             pltpu.VMEM((2, depth_all, tall, wide), f32),
-            pltpu.VMEM((depth_all, tall, wide), f32),
+            pltpu.VMEM((depth_all, rows, block), f32),
             pltpu.VMEM((srcs, 2, planes, rows, block), f32),
             pltpu.VMEM((srcs, 2, planes, rows, block), f32),
             dma((2,)), dma((2,)),
@@ -313,6 +372,7 @@
             dma((srcs - 1,)), dma((srcs - 1,)),
             dma((srcs - 1,)), dma((srcs - 1,)),
             dma((srcs - 1,)), dma((srcs - 1,)),
+            dma((srcs,)), dma((srcs,)),
         ],
         compiler_params=pltpu.CompilerParams(
             collective_id=0, has_side_effects=True, vmem_limit_bytes=40 * 1024 * 1024

time: 32.2 us -> 30.9 us (0.960)
  the two profiles are of different devices: /device:TPU:4 before, /device:TPU:0 now
where the time goes in v2:
time: 30.9 us; the launch traced here: 30.3 us
  Pallas kernels  25.8 us (83%)
  local copies, waits for them, and re-layouts  3.83 us (12%)
  between operations  0.67 us (2%)
    pallas_call x1, Pallas kernels, shards(): pl.pallas_call(functools.partial(kernel, dims), out_shape=(out, out), in_...  25.8 us
    unnamed x12, local copies, waits for them, and re-layouts  3.83 us

profile of v2, /device:TPU:0, one launch (start us, length us, event | category | flops | bytes accessed | tf_op | source)
XLA Modules:
  0.0 30.3 jit_solution(11614291094938539064)
XLA Ops:
  0.6 0.0 copy-start.4
  0.6 0.0 copy-start.3
  0.7 0.0 copy-start.2
  0.7 0.6 %copy-done.4 = f32[2]{0:T(128)S(1)} copy-done((f32[2]{0:T(128)S(1)}, f32[2]{0:T(128)}, u32[]{:S(2)}) %copy-start.4) | copy-done | bytes 32
  1.3 0.0 copy-done.3
  1.3 0.0 copy-done.2
  1.3 0.0 copy-start
  1.3 1.1 %copy-done = bf16[4,3,8,2,17,17]{5,3,4,2,1,0:T(2,128)(2,1)S(1)} copy-done((bf16[4,3,8,2,17,17]{5,3,4,2,1,0:T(2,128)(2,1)S(1)}, bf16[4,3,8,2,17,17]{5,3,4,2,1,0:T(2,128)(2,1)}, u32[]{:S(2)}) %copy-start) | copy-done | bytes 111000
  2.5 0.0 copy-start.1
  2.5 0.8 %copy-done.1 = s32[16,512]{1,0:T(8,128)S(1)} copy-done((s32[16,512]{1,0:T(8,128)S(1)}, s32[16,512]{1,0:T(8,128)}, u32[]{:S(2)}) %copy-start.1) | copy-done | bytes 32792
  3.2 25.8 %shard_map.68 = (f32[2,16,512]{2,1,0:T(8,128)S(1)}, f32[2,16,512]{2,1,0:T(8,128)S(1)}) custom-call(s32[16,512]{1,0:T(8,128)S(1)} %copy-done.1, bf16[3264,17]{1,0:T(8,128)(2,1)S(1)} %bitcast.3, s32[4]{0:T(128)S(1)} %copy-done.2, f32[2]{0:T(128)S(1)} %copy-done.3, f32[2]{0:T(128)S(1)} %copy-done.4), custom_call_target="tpu_custom_call" | custom-call | tf_op jit(solution)/shard_map/pallas_call | solution.py:342
  29.0 0.6 %copy.9 = f32[2,16,512]{2,1,0:T(8,128)} copy(f32[2,16,512]{2,1,0:T(8,128)S(1)} %get-tuple-element.4) | data formatting | bytes 131072
  29.6 0.6 %copy.10 = f32[2,16,512]{2,1,0:T(8,128)} copy(f32[2,16,512]{2,1,0:T(8,128)S(1)} %get-tuple-element.5) | data formatting | bytes 131072
Async XLA Ops:
  0.6 0.7 %copy-start.4 = (f32[2]{0:T(128)S(1)}, f32[2]{0:T(128)}, u32[]{:S(2)}) copy-start(f32[2]{0:T(128)} %quench_ref.1) | copy-start | bytes 28
  0.6 0.7 %copy-start.3 = (f32[2]{0:T(128)S(1)}, f32[2]{0:T(128)}, u32[]{:S(2)}) copy-start(f32[2]{0:T(128)} %dill_ref.1) | copy-start | bytes 28
  0.7 0.7 %copy-start.2 = (s32[4]{0:T(128)S(1)}, s32[4]{0:T(128)}, u32[]{:S(2)}) copy-start(s32[4]{0:T(128)} %pupil_ref.1) | copy-start | bytes 52
  1.3 1.1 %copy-start = (bf16[4,3,8,2,17,17]{5,3,4,2,1,0:T(2,128)(2,1)S(1)}, bf16[4,3,8,2,17,17]{5,3,4,2,1,0:T(2,128)(2,1)}, u32[]{:S(2)}) copy-start(bf16[4,3,8,2,17,17]{5,3,4,2,1,0:T(2,128)(2,1)} %param.6) | copy-start | bytes 332932
  2.5 0.8 %copy-start.1 = (s32[16,512]{1,0:T(8,128)S(1)}, s32[16,512]{1,0:T(8,128)}, u32[]{:S(2)}) copy-start(s32[16,512]{1,0:T(8,128)} %mask_ref.1) | copy-start | bytes 98308

commit v3 on v2

--- a/solution.py
+++ b/solution.py
@@ -25,11 +25,11 @@
 
 def kernel(
     dims,
-    mask_ref, raw_ref, pupil_ref, dill_ref, quench_ref, acid_ref, inhib_ref,
-    above, below, raw, unsorted, sorted_rows, filt_out, load_out, filters, loads, shifted, patches, taps,
+    mask_hbm, raw_hbm, pupil_hbm, dill_hbm, quench_hbm, out_hbm,
+    mask_ref, raw_ref, pupil_ref, dill_ref, quench_ref, above, below, raw, unsorted, sorted_rows, filt_out, load_out, filters, loads, shifted, patches, taps,
     light, light_out, light_in, rim_out, rim_in,
     acid, quench, dose, final_out, final_in,
-    mask_send, mask_recv, filt_send, filt_recv, load_send, load_recv,
+    here_sem, out_sem, mask_send, mask_recv, filt_send, filt_recv, load_send, load_recv,
     light_send, light_recv, rim_send, rim_recv, final_send, final_recv,
 ):
     tiles, srcs, rows, cols, side, planes, scale = dims
@@ -38,6 +38,14 @@
     tall = rows + 2 * halo
     block = cols // srcs
     wide = block + 128
+    local = [
+        pltpu.make_async_copy(there, here, here_sem.at[at])
+        for at, (there, here) in enumerate((
+            (raw_hbm, raw_ref), (pupil_hbm, pupil_ref), (quench_hbm, quench_ref),
+            (mask_hbm, mask_ref), (dill_hbm, dill_ref)))
+    ]
+    for copy in local:
+        copy.start()
     tile = lax.axis_index("tile")
     src = lax.axis_index("src")
     has_above = tile > 0
@@ -56,6 +64,10 @@
     def _():
         pl.semaphore_signal(barrier, inc=1, device_id=(tile + 1, src), device_id_type=MESH)
 
+    raw[...] = jnp.zeros_like(raw)
+    shifted[...] = jnp.zeros_like(shifted)
+    for copy in local:
+        copy.wait()
     lanes = 128
     points, parts = pupil_ref.shape[0], raw_ref.shape[0] // (2 * side * srcs * planes * pupil_ref.shape[0])
     channels = srcs * planes * points * parts
@@ -66,8 +78,6 @@
     for p in range(points):
         weight = jnp.where(point == p, pupil_ref[p].astype(jnp.float32), weight)
     weight = jnp.where(lane == lanes - 1, weight, 0.0)
-    raw[...] = jnp.zeros_like(raw)
-
     def widen(at, carry):
         here = pl.ds(pl.multiple_of(at * channels, channels), channels)
         raw[here, :side] = raw_ref[here, :].astype(jnp.float32)
@@ -136,7 +146,6 @@
         load_copies.append(copy)
     filters[src] = filt_out[src]
     loads[src] = load_out[...]
-    shifted[...] = jnp.zeros_like(shifted)
 
     @pl.when(jnp.logical_not(has_above))
     def _():
@@ -299,7 +308,7 @@
             reacted = react_rate * centre * quench[1, k, own, :block]
             a_next = blend(centre, sides, vertical, acid_lateral, acid_vertical) - reacted
             final_out[s, 0, k % planes] = a_next
-            final_out[s, 1, k % planes] = jnp.exp(-deprotect_rate * (dose[k] + a_next))
+            final_out[s, 1, k % planes] = dose[k] + a_next
 
         @pl.when(src != s)
         def _():
@@ -309,15 +318,22 @@
         def _():
             final_in[s] = final_out[s]
 
+    def place_copy(s):
+        return pltpu.make_async_copy(
+            final_in.at[s], out_hbm.at[:, :, :, s * block:(s + 1) * block], out_sem.at[s])
+
     for s in range(srcs):
         @pl.when(src != s)
         def _():
+            final_copy(s, s).wait_recv()
+
+        place_copy(s).start()
+    for s in range(srcs):
+        place_copy(s).wait()
+
+        @pl.when(src != s)
+        def _():
             final_copy(s, src).wait_send()
-            final_copy(s, s).wait_recv()
-
-    for s in range(srcs):
-        acid_ref[:, :, s * block:(s + 1) * block] = final_in[s, 0]
-        inhib_ref[:, :, s * block:(s + 1) * block] = final_in[s, 1]
 
 
 def shards(mask_tiles, kernels, source_weight, dill_rate, quencher_load):
@@ -335,16 +351,19 @@
     f32 = jnp.float32
     image_rows = 3 * rows
     deep_rows = max(image_rows * SLAB, (tall - GROUP) * SLAB + DEEP)
-    out = jax.ShapeDtypeStruct((planes, rows, cols), f32)
-    vmem = pl.BlockSpec(memory_space=pltpu.VMEM)
-    smem = pl.BlockSpec(memory_space=pltpu.SMEM)
+    out = jax.ShapeDtypeStruct((2, planes, rows, cols), f32)
     dma = pltpu.SemaphoreType.DMA
-    return pl.pallas_call(
+    result = pl.pallas_call(
         functools.partial(kernel, dims),
-        out_shape=(out, out),
-        in_specs=[vmem, vmem, smem, smem, smem],
-        out_specs=(vmem, vmem),
+        out_shape=out,
+        in_specs=[pl.BlockSpec(memory_space=pltpu.HBM)] * 5,
+        out_specs=pl.BlockSpec(memory_space=pl.ANY),
         scratch_shapes=[
+            pltpu.VMEM(mask_tiles.shape, jnp.int32),
+            pltpu.VMEM(raw.shape, jnp.bfloat16),
+            pltpu.SMEM(source_weight.shape, jnp.int32),
+            pltpu.SMEM(dill_rate.shape, f32),
+            pltpu.SMEM(quencher_load.shape, f32),
             pltpu.VMEM((rows, cols), jnp.int32),
             pltpu.VMEM((rows, cols), jnp.int32),
             pltpu.VMEM((raw.shape[0], 128), f32),
@@ -367,7 +386,7 @@
             pltpu.VMEM((depth_all, rows, block), f32),
             pltpu.VMEM((srcs, 2, planes, rows, block), f32),
             pltpu.VMEM((srcs, 2, planes, rows, block), f32),
-            dma((2,)), dma((2,)),
+            dma((5,)), dma((srcs,)), dma((2,)), dma((2,)),
             dma((srcs - 1,)), dma((srcs - 1,)),
             dma((srcs - 1,)), dma((srcs - 1,)),
             dma((srcs - 1,)), dma((srcs - 1,)),
@@ -375,9 +394,10 @@
             dma((srcs,)), dma((srcs,)),
         ],
         compiler_params=pltpu.CompilerParams(
-            collective_id=0, has_side_effects=True, vmem_limit_bytes=40 * 1024 * 1024
+            collective_id=0, has_side_effects=True, vmem_limit_bytes=60 * 1024 * 1024
         ),
     )(mask_tiles, raw, source_weight, dill_rate, quencher_load)
+    return result[0], jnp.exp(-deprotect_rate * result[1])
 
 
 def solution(mesh):

time: 30.9 us -> 29.5 us (0.955); the launches traced: 30.3 us -> 29.4 us
  local copies, waits for them, and re-layouts: 3.83 us -> 0 us
  other arithmetic: 0 us -> 1.54 us
  Pallas kernels: 25.8 us -> 27.2 us
    unnamed x12 -> x0, local copies, waits for them, and re-layouts: 3.83 us -> none
    exp x0 -> x1, other arithmetic: none -> 1.54 us  [shards(): return (result[0], jnp.exp(-deprotect_rate * result[1]))]
    pallas_call x1, Pallas kernels: 25.8 us -> 27.2 us  [shards(): pl.pallas_call(functools.partial(kernel, dims), out_shape=out, in_specs=[...]
where the time goes in v3:
time: 29.5 us; the launch traced here: 29.4 us
  Pallas kernels  27.2 us (92%)
  other arithmetic  1.54 us (5%)
  between operations  0.64 us (2%)
    pallas_call x1, Pallas kernels, shards(): pl.pallas_call(functools.partial(kernel, dims), out_shape=out, in_specs=[...  27.2 us
    exp x1, other arithmetic, shards(): return (result[0], jnp.exp(-deprotect_rate * result[1]))  1.54 us

profile of v3, /device:TPU:0, one launch (start us, length us, event | category | flops | bytes accessed | tf_op | source)
XLA Modules:
  0.0 29.4 jit_solution(1391942325332161685)
XLA Ops:
  0.6 27.2 %shard_map.68 = f32[2,2,16,512]{3,2,1,0:T(8,128)} custom-call(s32[16,512]{1,0:T(8,128)} %mask_hbm.1, bf16[3264,17]{1,0:T(8,128)(2,1)} %bitcast.7, s32[4]{0:T(128)} %pupil_hbm.1, f32[2]{0:T(128)} %dill_hbm.1, f32[2]{0:T(128)} %quench_hbm.1), custom_call_target="tpu_custom_call" | custom-call | tf_op jit(solution)/shard_map/pallas_call | solution.py:356
  27.8 1.5 %exponential_bitcast_fusion = (f32[2,16,512]{2,1,0:T(8,128)}, f32[2,16,512]{2,1,0:T(8,128)}) fusion(f32[2,2,16,512]{3,2,1,0:T(8,128)} %shard_map.68), kind=kLoop, calls=%fused_computation | loop fusion | flops 16384 | bytes 262144 | tf_op jit(solution)/shard_map/exp | solution.py:400

commit v4 on v3

--- a/solution.py
+++ b/solution.py
@@ -179,6 +179,32 @@
                 c, g * GROUP * SLAB:g * GROUP * SLAB + DEEP, :].astype(jnp.bfloat16)
     light[...] = jnp.zeros_like(light)
 
+    half = tall // 2
+    edge = lax.broadcasted_iota(jnp.int32, (GROUP, 128), 1)
+    none = jnp.zeros((GROUP, 128), jnp.float32)
+    rims = [none] * srcs
+    copies = []
+
+    def ship(h):
+        for k in range(planes):
+            exposed = light[k, h * half:(h + 1) * half] * (dill_ref[k] * scale)
+            for s in range(srcs):
+                light_out[h, s, k] = exposed[:, s * block:(s + 1) * block].astype(jnp.bfloat16)
+                for g in range(half // GROUP):
+                    rows8 = exposed[g * GROUP:(g + 1) * GROUP]
+                    right = rows8[:, (s + 1) * block:(s + 1) * block + 128] if s < srcs - 1 else none
+                    left = rows8[:, s * block - 128:s * block] if s else none
+                    picked = jnp.where(edge < halo, right, jnp.where(edge >= 128 - halo, left, 0.0))
+                    shift = 2 * halo * (k * (tall // GROUP) + h * (half // GROUP) + g)
+                    rims[s] = rims[s] + (pltpu.roll(picked, shift, 1) if shift else picked)
+        for at, peer in enumerate(peers):
+            copy = pltpu.make_async_remote_copy(
+                light_out.at[h, peer], light_in.at[h, src], light_send.at[h, at], light_recv.at[h, at],
+                device_id=(tile, peer), device_id_type=MESH)
+            copy.start()
+            copies.append(copy)
+        light_in[h, src] = light_out[h, src]
+
     place = lax.broadcasted_iota(jnp.int32, (2 * share, WIRE), 1)
     ours = lax.broadcasted_iota(jnp.int32, (share, cols), 0) // (points * parts)
     for step in range(srcs):
@@ -192,52 +218,29 @@
             moved = pltpu.roll(held, r * SLAB, 1) if r else held
             taps[r * 2 * share:(r + 1) * 2 * share] = moved.astype(jnp.bfloat16)
 
-        def one_group(g, carry):
+        for g in range(tall // GROUP):
             field = jnp.dot(taps[...], patches[g], preferred_element_type=jnp.float32)
             square = (field * field).reshape(GROUP, 2, share, cols)
             power = (square[:, 0] + square[:, 1]) * weights
-            start = pl.multiple_of(g * GROUP, GROUP)
             for k in range(planes):
                 own = jnp.where(ours == k, power, 0.0)
-                light[k, pl.ds(start, GROUP), :] += jnp.sum(own, axis=1)
-            return carry
-
-        lax.fori_loop(0, tall // GROUP, one_group, 0)
-    for copy in load_copies:
-        copy.wait()
-    for copy in filt_copies:
-        copy.wait_send()
-
-    edge = lax.broadcasted_iota(jnp.int32, (GROUP, 128), 1)
-    none = jnp.zeros((GROUP, 128), jnp.float32)
-    rims = [none] * srcs
-    for k in range(planes):
-        exposed = light[k] * (dill_ref[k] * scale)
-        for s in range(srcs):
-            light_out[s, k] = exposed[:, s * block:(s + 1) * block].astype(jnp.bfloat16)
-            for g in range(tall // GROUP):
-                rows8 = exposed[g * GROUP:(g + 1) * GROUP]
-                right = rows8[:, (s + 1) * block:(s + 1) * block + 128] if s < srcs - 1 else none
-                left = rows8[:, s * block - 128:s * block] if s else none
-                picked = jnp.where(edge < halo, right, jnp.where(edge >= 128 - halo, left, 0.0))
-                shift = 2 * halo * (k * (tall // GROUP) + g)
-                rims[s] = rims[s] + (pltpu.roll(picked, shift, 1) if shift else picked)
+                light[k, g * GROUP:(g + 1) * GROUP] += jnp.sum(own, axis=1)
+            if step == srcs - 1 and (g + 1) * GROUP % half == 0:
+                ship(g * GROUP // half)
     for s in range(srcs):
         rim_out[s] = rims[s]
-    copies = []
     for at, peer in enumerate(peers):
-        copy = pltpu.make_async_remote_copy(
-            light_out.at[peer], light_in.at[src], light_send.at[at], light_recv.at[at],
-            device_id=(tile, peer), device_id_type=MESH)
-        copy.start()
-        copies.append(copy)
         copy = pltpu.make_async_remote_copy(
             rim_out.at[peer], rim_in.at[src], rim_send.at[at], rim_recv.at[at],
             device_id=(tile, peer), device_id_type=MESH)
         copy.start()
         copies.append(copy)
-    light_in[src] = light_out[src]
     rim_in[src] = rim_out[src]
+    for copy in load_copies:
+        copy.wait()
+    for copy in filt_copies:
+        copy.wait_send()
+
     row = lax.broadcasted_iota(jnp.int32, (tall, wide), 0) + (tile * rows - halo)
     col = lax.broadcasted_iota(jnp.int32, (tall, wide), 1)
     col = src * block + jnp.where(col < block + 64, col, col - wide)
@@ -253,8 +256,9 @@
         for g in range(tall // GROUP):
             shift = 2 * halo * (k % planes * (tall // GROUP) + g)
             rim.append(pltpu.roll(sent, 128 - shift, 1) if shift else sent)
+        main = jnp.concatenate([light_in[h, k // planes, k % planes] for h in range(2)], axis=0)
         exposed = jnp.concatenate(
-            [light_in[k // planes, k % planes].astype(jnp.float32), jnp.concatenate(rim, axis=0)], axis=1)
+            [main.astype(jnp.float32), jnp.concatenate(rim, axis=0)], axis=1)
         acid[0, k] = (1.0 - jnp.exp(-exposed)) * inside
         quench[0, k] = loads[k // planes, k % planes:k % planes + 1, 0:1] * inside
         dose[k] = jnp.zeros((rows, block), jnp.float32)
@@ -377,8 +381,8 @@
             pltpu.VMEM((tall // GROUP, DEEP, cols), jnp.bfloat16),
             pltpu.VMEM((GROUP * 2 * share, DEEP), jnp.bfloat16),
             pltpu.VMEM((planes, tall, cols), f32),
-            pltpu.VMEM((srcs, planes, tall, block), jnp.bfloat16),
-            pltpu.VMEM((srcs, planes, tall, block), jnp.bfloat16),
+            pltpu.VMEM((2, srcs, planes, tall // 2, block), jnp.bfloat16),
+            pltpu.VMEM((2, srcs, planes, tall // 2, block), jnp.bfloat16),
             pltpu.VMEM((srcs, GROUP, 128), f32),
             pltpu.VMEM((srcs, GROUP, 128), f32),
             pltpu.VMEM((2, depth_all, tall, wide), f32),
@@ -389,7 +393,7 @@
             dma((5,)), dma((srcs,)), dma((2,)), dma((2,)),
             dma((srcs - 1,)), dma((srcs - 1,)),
             dma((srcs - 1,)), dma((srcs - 1,)),
-            dma((srcs - 1,)), dma((srcs - 1,)),
+            dma((2, srcs - 1)), dma((2, srcs - 1)),
             dma((srcs - 1,)), dma((srcs - 1,)),
             dma((srcs,)), dma((srcs,)),
         ],

time: 29.5 us -> 27.2 us (0.922)
  Pallas kernels: 27.2 us -> 24.8 us
    pallas_call x1, Pallas kernels: 27.2 us -> 24.8 us  [shards(): pl.pallas_call(functools.partial(kernel, dims), out_shape=out, in_specs=[...]
where the time goes in v4:
time: 27.2 us; the launch traced here: 27 us
  Pallas kernels  24.8 us (91%)
  other arithmetic  1.54 us (6%)
  between operations  0.64 us (2%)
    pallas_call x1, Pallas kernels, shards(): pl.pallas_call(functools.partial(kernel, dims), out_shape=out, in_specs=[...  24.8 us
    exp x1, other arithmetic, shards(): return (result[0], jnp.exp(-deprotect_rate * result[1]))  1.54 us

profile of v4, /device:TPU:0, one launch (start us, length us, event | category | flops | bytes accessed | tf_op | source)
XLA Modules:
  0.0 27.0 jit_solution(15074800092471229068)
XLA Ops:
  0.6 24.8 %shard_map.68 = f32[2,2,16,512]{3,2,1,0:T(8,128)} custom-call(s32[16,512]{1,0:T(8,128)} %mask_hbm.1, bf16[3264,17]{1,0:T(8,128)(2,1)} %bitcast.7, s32[4]{0:T(128)} %pupil_hbm.1, f32[2]{0:T(128)} %dill_hbm.1, f32[2]{0:T(128)} %quench_hbm.1), custom_call_target="tpu_custom_call" | custom-call | tf_op jit(solution)/shard_map/pallas_call | solution.py:360
  25.5 1.5 %exponential_bitcast_fusion = (f32[2,16,512]{2,1,0:T(8,128)}, f32[2,16,512]{2,1,0:T(8,128)}) fusion(f32[2,2,16,512]{3,2,1,0:T(8,128)} %shard_map.68), kind=kLoop, calls=%fused_computation | loop fusion | flops 16384 | bytes 262144 | tf_op jit(solution)/shard_map/exp | solution.py:404

commit v5 on v4

--- a/solution.py
+++ b/solution.py
@@ -83,7 +83,7 @@
         raw[here, :side] = raw_ref[here, :].astype(jnp.float32)
         return carry
 
-    lax.fori_loop(0, 2 * side, widen, 0)
+    lax.fori_loop(0, 2 * side, widen, 0, unroll=True)
     for q in range(2):
         strips = [jnp.zeros((channels, lanes), jnp.float32) for _ in range(WIRE // lanes)]
         strips[-1] = weight

time: 27.2 us -> 26.8 us (0.985)
  Pallas kernels: 24.8 us -> 24.5 us
    pallas_call x1, Pallas kernels: 24.8 us -> 24.5 us  [shards(): pl.pallas_call(functools.partial(kernel, dims), out_shape=out, in_specs=[...]
where the time goes in v5:
time: 26.8 us; the launch traced here: 26.6 us
  Pallas kernels  24.5 us (91%)
  other arithmetic  1.54 us (6%)
  between operations  0.64 us (2%)
    pallas_call x1, Pallas kernels, shards(): pl.pallas_call(functools.partial(kernel, dims), out_shape=out, in_specs=[...  24.5 us
    exp x1, other arithmetic, shards(): return (result[0], jnp.exp(-deprotect_rate * result[1]))  1.54 us

profile of v5, /device:TPU:0, one launch (start us, length us, event | category | flops | bytes accessed | tf_op | source)
XLA Modules:
  0.0 26.6 jit_solution(17943208499964614992)
XLA Ops:
  0.6 24.5 %shard_map.68 = f32[2,2,16,512]{3,2,1,0:T(8,128)} custom-call(s32[16,512]{1,0:T(8,128)} %mask_hbm.1, bf16[3264,17]{1,0:T(8,128)(2,1)} %bitcast.7, s32[4]{0:T(128)} %pupil_hbm.1, f32[2]{0:T(128)} %dill_hbm.1, f32[2]{0:T(128)} %quench_hbm.1), custom_call_target="tpu_custom_call" | custom-call | tf_op jit(solution)/shard_map/pallas_call | solution.py:360
  25.1 1.5 %exponential_bitcast_fusion = (f32[2,16,512]{2,1,0:T(8,128)}, f32[2,16,512]{2,1,0:T(8,128)}) fusion(f32[2,2,16,512]{3,2,1,0:T(8,128)} %shard_map.68), kind=kLoop, calls=%fused_computation | loop fusion | flops 16384 | bytes 262144 | tf_op jit(solution)/shard_map/exp | solution.py:404
